TPU v7x, 32 devices: a whole 2x2x4 slice. The times are simulated.
32 devices in a mesh: clu: 32 (over z, y, x, core).
Axes of the slice: x: 2, y: 2, z: 4, core: 2. Of those that a mesh axis runs over, the one named last changes fastest.
Arguments:
- right_sides: float32 [32768, 256], P('clu'), may hold values from -6 to 6
- diag_shift: float32 [32768], P('clu'), may hold values from 1.5 to 3
- near_block: float32 [32768, 1024], P('clu')
- cluster_basis: float32 [32768, 512], P('clu'), may hold values from -0.1875 to 0.1875
- couplings: float32 [192, 512, 512], P('clu'), may hold values from -0.015625 to 0.015625
- partner: int32 [32, 6], P('clu'), may hold values from 1 to 31, as said below
- owned_count: int32 [32], P('clu'), may hold values from 0 to 6, as said below
Outputs:
- solution: float32 [32768, 256], P('clu')
- residual: float32 [32768, 256], P('clu')
Inputs may be any that keep to these rules, and one draw needn't show every extreme that they name: `partner`: slots of cluster c below owned_count[c] name distinct clusters c+1 to c+8, ascending; later slots are unused. `owned_count`: cluster 0 owns 6 live slots; the last cluster owns none.
All inputs are finite; a program needn't handle non-finite values.
Results may differ from a plain program's by a relative error of at most 0.0003.
Values sent between devices are 32-bit elements; how exact they have to be, the bound alone decides.
A program may use at most 128 MiB of HBM per device.

v0:
```python
import functools

import jax
import jax.numpy as jnp
from jax import lax
from jax.experimental import pallas as pl
from jax.experimental.pallas import tpu as pltpu
from jax.sharding import PartitionSpec as P

GROUP = 8
MESH = pl.DeviceIdType.MESH
VMEM_LIMIT = 56 * 1024 * 1024

highest = lax.Precision.HIGHEST
high = lax.Precision.HIGH
contract_first = (((0,), (0,)), ((), ()))
contract_last = (((1,), (1,)), ((), ()))
plain = (((1,), (0,)), ((), ()))


def split(x):
    hi = x.astype(jnp.bfloat16)
    return hi, (x - hi.astype(jnp.float32)).astype(jnp.bfloat16)


def dot3(a, b, dims):
    a_hi, a_lo = a
    b_hi, b_lo = b
    d = functools.partial(
        lax.dot_general, dimension_numbers=dims, preferred_element_type=jnp.float32
    )
    return d(a_hi, b_hi) + (d(a_hi, b_lo) + d(a_lo, b_hi))


def far_kernel(n, meta, coef, c_hbm, out, cv, ahead, ret, rs, ri, up, rz,
               c_sem, fs, fr, ss, sr, xs, xr, zs, zr):
    me = lax.axis_index("clu")
    z = me // GROUP
    p = me % GROUP
    a = p // 2
    k = p % 2
    base = z * GROUP
    has_up = z < n // GROUP - 1
    has_down = z > 0
    sib = base + (p + 1 - 2 * k)
    psib = p + 1 - 2 * k
    slots = cv.shape[0]

    def chip(i):
        x, y = a % 2, a // 2
        nx = 1 - x if i & 1 else x
        ny = 1 - y if i & 2 else y
        return ny * 2 + nx

    chips = {i: chip(i) for i in (1, 2, 3)}

    def rc(src, dst, ssem, rsem, dev):
        return pltpu.make_async_remote_copy(
            src_ref=src, dst_ref=dst, send_sem=ssem, recv_sem=rsem,
            device_id=(dev,), device_id_type=MESH)

    c_copy = pltpu.make_async_copy(c_hbm, cv, c_sem)
    c_copy.start()

    @pl.when(jnp.logical_not(has_up))
    def _():
        def zero(j, c):
            ahead[j] = jnp.zeros(ahead.shape[1:], jnp.float32)
            return c
        lax.fori_loop(0, GROUP, zero, 0)

    barrier = pltpu.get_barrier_semaphore()
    pl.semaphore_signal(barrier, inc=1, device_id=(sib,), device_id_type=MESH)
    for i in (1, 2, 3):
        pl.semaphore_signal(barrier, inc=1, device_id=(base + chips[i] * 2 + k,), device_id_type=MESH)

    @pl.when(has_up)
    def _():
        pl.semaphore_signal(barrier, inc=1, device_id=(me + GROUP,), device_id_type=MESH)

    @pl.when(has_down)
    def _():
        pl.semaphore_signal(barrier, inc=1, device_id=(me - GROUP,), device_id_type=MESH)

    pl.semaphore_wait(barrier, 4 + jnp.where(has_up, 1, 0) + jnp.where(has_down, 1, 0))

    f_z = rc(coef, ahead.at[p], fs.at[0], fr.at[0], me - GROUP)

    def f_own(i):
        return rc(coef, ahead.at[p], fs.at[i], fr.at[i], base + chips[i] * 2 + k)

    def f_upper(i):
        return rc(ahead.at[p], ahead.at[p], fs.at[i], fr.at[i], base + chips[i] * 2 + k)

    def f_in(i):
        t = chips[i] * 2 + k
        return rc(ahead.at[t], ahead.at[t], fs.at[3 + i], fr.at[i], sib)

    def f_sib(i):
        t = chips[i] * 2 + k
        return rc(ahead.at[t], ahead.at[t], fs.at[3 + i], fr.at[3 + i], sib)

    def f_sib_in(i):
        t = chips[i] * 2 + 1 - k
        return rc(ahead.at[t], ahead.at[t], fs.at[3 + i], fr.at[3 + i], sib)

    f_s_own = rc(coef, ahead.at[p], fs.at[7], fr.at[7], sib)
    f_s_upper = rc(ahead.at[p], ahead.at[p], fs.at[7], fr.at[7], sib)
    f_s_in = rc(ahead.at[psib], ahead.at[psib], fs.at[7], fr.at[7], sib)

    @pl.when(has_down)
    def _():
        f_z.start()

    for i in (3, 1, 2):
        @pl.when(chips[i] < a)
        def _(i=i):
            f_own(i).start()

    @pl.when(k == 1)
    def _():
        f_s_own.start()

    c_copy.wait()

    def back(t, carry):
        s = meta[0, t]
        term = dot3(split(coef[...]), split(cv[s]), plain)
        ret[t] = jnp.where(meta[1, t] > 0, term, 0.0)
        return carry

    lax.fori_loop(0, GROUP, back, 0)

    r_s = [rc(ret.at[psib], rs.at[0], ss.at[0], sr.at[0], sib)]
    for i in (1, 2, 3):
        r_s.append(rc(ret.at[chips[i] * 2 + 1 - k], rs.at[i], ss.at[i], sr.at[i], sib))
    for i in (3, 1, 2, 0):
        r_s[i].start()

    @pl.when(has_up)
    def _():
        f_z.wait_recv()
        for i in (3, 1, 2):
            @pl.when(chips[i] > a)
            def _(i=i):
                f_upper(i).start()

        @pl.when(k == 0)
        def _():
            f_s_upper.start()

    r_x = [None]
    for i in (1, 2, 3):
        r_x.append(rc(ret.at[chips[i] * 2 + k], ri.at[i - 1], xs.at[i - 1], xr.at[i - 1],
                      base + chips[i] * 2 + k))
    for i in (3, 1, 2):
        r_s[i].wait_recv()
        t = chips[i] * 2 + k
        ret[t] = ret[t] + rs[i]
        r_x[i].start()

    for i in (1, 2, 3):
        @pl.when(jnp.logical_or(chips[i] > a, has_up))
        def _(i=i):
            f_in(i).wait_recv()
            f_sib(i).start()

    r_s[0].wait_recv()
    up[...] = ret[p] + jnp.where(k == 0, rs[0], 0.0)
    out[...] = jnp.where(k == 0, 0.0, rs[0])
    for i in (1, 2, 3):
        r_x[i].wait_recv()
        mine = chips[i] < a
        got = ri[i - 1]
        up[...] += jnp.where(mine, 0.0, got)
        out[...] += jnp.where(mine, got, 0.0)
    r_z = rc(up, rz, zs, zr, me + GROUP)

    @pl.when(has_up)
    def _():
        r_z.start()

    for i in (1, 2, 3):
        @pl.when(jnp.logical_or(chips[i] > a, has_up))
        def _(i=i):
            f_sib_in(i).wait_recv()

    @pl.when(jnp.logical_or(k == 0, has_up))
    def _():
        f_s_in.wait_recv()

    def forth(s, carry):
        block = ahead[meta[2, s]]
        term = dot3(split(block), split(cv[s]), contract_last)
        out[...] += jnp.where(meta[3, s] > 0, term, 0.0)
        return carry

    lax.fori_loop(0, slots, forth, 0)

    @pl.when(has_down)
    def _():
        r_z.wait_recv()
        out[...] += rz[...]
        f_z.wait_send()

    for i in (1, 2, 3):
        @pl.when(jnp.logical_or(chips[i] < a, has_up))
        def _(i=i):
            f_own(i).wait_send()

        @pl.when(jnp.logical_or(chips[i] > a, has_up))
        def _(i=i):
            f_sib(i).wait_send()

        r_x[i].wait_send()
    for i in range(4):
        r_s[i].wait_send()

    @pl.when(jnp.logical_or(k == 1, has_up))
    def _():
        f_s_own.wait_send()

    @pl.when(has_up)
    def _():
        r_z.wait_send()


def far_exchange(n, meta, coef_t, couplings):
    blk = coef_t.shape
    f32 = jnp.float32
    return pl.pallas_call(
        functools.partial(far_kernel, n),
        out_shape=jax.ShapeDtypeStruct(blk, f32),
        in_specs=[
            pl.BlockSpec(memory_space=pltpu.SMEM),
            pl.BlockSpec(memory_space=pltpu.VMEM),
            pl.BlockSpec(memory_space=pl.ANY),
        ],
        out_specs=pl.BlockSpec(memory_space=pltpu.VMEM),
        scratch_shapes=[
            pltpu.VMEM(couplings.shape, f32),
            pltpu.VMEM((GROUP,) + blk, f32),
            pltpu.VMEM((GROUP,) + blk, f32),
            pltpu.VMEM((4,) + blk, f32),
            pltpu.VMEM((3,) + blk, f32),
            pltpu.VMEM(blk, f32),
            pltpu.VMEM(blk, f32),
            pltpu.SemaphoreType.DMA,
            pltpu.SemaphoreType.DMA((8,)),
            pltpu.SemaphoreType.DMA((8,)),
            pltpu.SemaphoreType.DMA((4,)),
            pltpu.SemaphoreType.DMA((4,)),
            pltpu.SemaphoreType.DMA((3,)),
            pltpu.SemaphoreType.DMA((3,)),
            pltpu.SemaphoreType.DMA,
            pltpu.SemaphoreType.DMA,
        ],
        compiler_params=pltpu.CompilerParams(
            collective_id=0, has_side_effects=True, vmem_limit_bytes=VMEM_LIMIT),
        name="far_exchange",
    )(meta, coef_t, couplings)


def sum_kernel(n, g, out, inbox, planes, s1, r1, s2, r2, s3, r3):
    me = lax.axis_index("clu")
    z = me // GROUP
    p = me % GROUP
    base = z * GROUP
    groups = n // GROUP
    rows = g.shape[0] // GROUP

    barrier = pltpu.get_barrier_semaphore()
    for j in range(1, GROUP):
        pl.semaphore_signal(barrier, inc=1, device_id=(base + (p + j) % GROUP,), device_id_type=MESH)
    for j in range(1, groups):
        pl.semaphore_signal(barrier, inc=1, device_id=((me + j * GROUP) % n,), device_id_type=MESH)
    pl.semaphore_wait(barrier, GROUP - 1 + groups - 1)

    def rc(src, dst, ssem, rsem, dev):
        return pltpu.make_async_remote_copy(
            src_ref=src, dst_ref=dst, send_sem=ssem, recv_sem=rsem,
            device_id=(dev,), device_id_type=MESH)

    def part(t):
        return pl.ds(pl.multiple_of(t * rows, 8), rows)

    scatter = []
    for j in range(1, GROUP):
        t = (p + j) % GROUP
        scatter.append(rc(g.at[part(t)], inbox.at[j - 1], s1.at[j - 1], r1.at[j - 1], base + t))
        scatter[-1].start()
    total = g[part(p), :]
    for j in range(1, GROUP):
        scatter[j - 1].wait_recv()
        total = total + inbox[j - 1]
    planes[z] = total
    across = []
    for j in range(1, groups):
        across.append(rc(planes.at[z], planes.at[z], s2.at[j - 1], r2.at[j - 1], (me + j * GROUP) % n))
        across[-1].start()
    for j in range(1, groups):
        src = (z + groups - j) % groups
        rc(planes.at[src], planes.at[src], s2.at[j - 1], r2.at[j - 1], (me + j * GROUP) % n).wait_recv()
    total = planes[0]
    for j in range(1, groups):
        total = total + planes[j]
    out[part(p), :] = total
    gather = []
    for j in range(1, GROUP):
        t = (p + j) % GROUP
        gather.append(rc(out.at[part(p)], out.at[part(p)], s3.at[j - 1], r3.at[j - 1], base + t))
        gather[-1].start()
    for j in range(1, GROUP):
        t = (p + GROUP - j) % GROUP
        rc(out.at[part(t)], out.at[part(t)], s3.at[j - 1], r3.at[j - 1], base + t).wait_recv()
    for copy in scatter + across + gather:
        copy.wait_send()


def sum_all(n, g, collective_id):
    rows = g.shape[0] // GROUP
    groups = n // GROUP
    f32 = jnp.float32
    return pl.pallas_call(
        functools.partial(sum_kernel, n),
        out_shape=jax.ShapeDtypeStruct(g.shape, f32),
        in_specs=[pl.BlockSpec(memory_space=pltpu.VMEM)],
        out_specs=pl.BlockSpec(memory_space=pltpu.VMEM),
        scratch_shapes=[
            pltpu.VMEM((GROUP - 1, rows, g.shape[1]), f32),
            pltpu.VMEM((groups, rows, g.shape[1]), f32),
            pltpu.SemaphoreType.DMA((GROUP - 1,)),
            pltpu.SemaphoreType.DMA((GROUP - 1,)),
            pltpu.SemaphoreType.DMA((groups - 1,)),
            pltpu.SemaphoreType.DMA((groups - 1,)),
            pltpu.SemaphoreType.DMA((GROUP - 1,)),
            pltpu.SemaphoreType.DMA((GROUP - 1,)),
        ],
        compiler_params=pltpu.CompilerParams(
            collective_id=collective_id, has_side_effects=True, vmem_limit_bytes=VMEM_LIMIT),
        name="sum_all_%d" % g.shape[0],
    )(g)


def mm(x, y, dims=plain):
    return lax.dot_general(x, y, dims, precision=highest, preferred_element_type=jnp.float32)


def invert_blocks(mats):
    size = mats[0].shape[0]
    lane = lax.broadcasted_iota(jnp.int32, (1, size), 1)
    sub = lax.broadcasted_iota(jnp.int32, (size, 1), 0)
    mats = list(mats)
    for step in range(size):
        for m, mat in enumerate(mats):
            row = mat[step:step + 1, :]
            col = mat[:, step:step + 1]
            inv = 1.0 / mat[step:step + 1, step:step + 1]
            scaled = jnp.where(lane == step, inv, row * inv)
            factor = jnp.where(sub == step, -1.0, col)
            kept = jnp.where(jnp.logical_or(lane == step, sub == step), 0.0, mat)
            mats[m] = kept - factor * scaled
    return mats


def invert(mats):
    half = mats[0].shape[0] // 2
    a = [m[:half, :half] for m in mats]
    b = [m[:half, half:] for m in mats]
    d = [m[half:, half:] for m in mats]
    ai = invert_blocks(a)
    ab = [mm(x, y) for x, y in zip(ai, b)]
    si = invert_blocks([x - mm(y, w, contract_first) for x, y, w in zip(d, b, ab)])
    result = []
    for x, y, w in zip(ai, ab, si):
        yw = mm(y, w)
        top = jnp.concatenate([x + mm(yw, y, contract_last), -yw], axis=1)
        low = jnp.concatenate([-jnp.transpose(yw), w], axis=1)
        result.append(jnp.concatenate([top, low], axis=0))
    return result


def symmetric(matrix):
    return 0.5 * (matrix + jnp.transpose(matrix))


def first_kernel(grams, alpha_ref, beta_ref):
    size = grams.shape[1]
    g0 = symmetric(grams[:size, :])
    g1 = symmetric(grams[size:2 * size, :])
    g2 = symmetric(grams[2 * size:, :])
    i0, i1 = invert([g0, g1])
    alpha = mm(i1, g0)
    alpha_ref[...] = alpha
    inner = mm(g2, alpha) - g1
    cross = mm(g1, alpha)
    updated = symmetric((g0 - cross) + mm(alpha, inner, contract_first))
    beta_ref[...] = mm(i0, updated)


def second_kernel(curv, cur, alpha_ref):
    (inverse,) = invert([symmetric(curv[...])])
    alpha_ref[...] = mm(inverse, cur[...])


def local_call(kernel, out_shapes, name, *args):
    return pl.pallas_call(
        kernel,
        out_shape=out_shapes,
        compiler_params=pltpu.CompilerParams(vmem_limit_bytes=VMEM_LIMIT),
        name=name,
    )(*args)


def per_device(n, right_sides, diag_shift, near_block, cluster_basis, couplings, partner, owned_count):
    cols = right_sides.shape[1]
    square = jax.ShapeDtypeStruct((cols, cols), jnp.float32)
    slots = partner.shape[1]
    live = jnp.arange(slots) < owned_count[0]
    where_to = partner[0] % GROUP
    match = jnp.logical_and(live[None, :], where_to[None, :] == jnp.arange(GROUP)[:, None])
    pad = [(0, GROUP - slots)]
    meta = jnp.stack([
        jnp.argmax(match, axis=1).astype(jnp.int32),
        jnp.any(match, axis=1).astype(jnp.int32),
        jnp.pad(where_to.astype(jnp.int32), pad),
        jnp.pad(live.astype(jnp.int32), pad),
    ])

    def image_of(vectors):
        coef_t = lax.dot_general(vectors, cluster_basis, contract_first, precision=high)
        near = jnp.dot(near_block, vectors, precision=high)
        far_t = far_exchange(n, meta, coef_t, couplings)
        far = lax.dot_general(cluster_basis, far_t, contract_last, precision=high)
        return diag_shift[:, None] * vectors + (near + far)

    def gram(x, y):
        return lax.dot_general(x, y, contract_first, precision=highest)

    image = image_of(right_sides)
    local = jnp.concatenate([
        gram(right_sides, right_sides), gram(right_sides, image), gram(image, image)])
    grams = sum_all(n, local, 1)
    alpha, beta = local_call(first_kernel, (square, square), "first_steps", grams)
    residual = right_sides - jnp.dot(image, alpha, precision=highest)
    direction = residual + jnp.dot(right_sides, beta, precision=highest)
    image2 = image_of(direction)
    both = jnp.concatenate([gram(direction, image2), gram(residual, residual)])
    summed = sum_all(n, both, 2)
    alpha2 = local_call(second_kernel, square, "second_step", summed[:cols], symmetric(summed[cols:]))
    answer = jnp.dot(right_sides, alpha, precision=highest) + jnp.dot(direction, alpha2, precision=highest)
    residual = residual - jnp.dot(image2, alpha2, precision=highest)
    return answer, residual


def solution(mesh):
    n = mesh.shape["clu"]
    in_specs = (
        P("clu", None),
        P("clu"),
        P("clu", None),
        P("clu", None),
        P("clu", None, None),
        P("clu", None),
        P("clu"),
    )
    out_specs = (P("clu", None), P("clu", None))
    return jax.shard_map(
        functools.partial(per_device, n), mesh=mesh, in_specs=in_specs,
        out_specs=out_specs, check_vma=False)
```

profile of v0, /device:TPU:0, one launch (start us, length us, event | category | flops | bytes accessed | tf_op | source)
XLA Modules:
  0.0 323.8 jit_solution(13851178324386571154)
XLA Ops:
  1.5 0.8 fusion.8
  2.4 0.7 and_select_fusion
  3.1 0.6 iota_reduce_fusion
  3.7 0.6 pad_add_fusion.meta
  4.3 3.4 %fusion.12 = f32[256,256]{1,0:T(8,128)S(1)} fusion(f32[1024,256]{1,0:T(8,128)} %param.7), kind=kOutput, calls=%fused_computation.36 | convolution fusion | flops 805306368 | bytes 1310720 | tf_op jit(solution)/shard_map/dot_general | solution.py:438
  7.7 1.8 fusion.13.coef
  9.5 63.8 %far_exchange.2 = f32[256,512]{1,0:T(8,128)} custom-call(s32[4,8]{1,0:T(4,128)} %pad_add_fusion.meta, f32[256,512]{1,0:T(8,128)} %fusion.13.coef, f32[6,512,512]{2,1,0:T(8,128)} %c_hbm.3), custom_call_target="tpu_custom_call" | custom-call | tf_op jit(solution)/shard_map/far_exchange/pallas_call | solution.py:231
  73.3 2.1 convolution_bitcast_fusion
  75.5 4.0 %fusion.2 = f32[1024,256]{1,0:T(8,128)S(1)} fusion(f32[1024,256]{1,0:T(8,128)S(1)} %convolution_bitcast_fusion, f32[1024,1024]{1,0:T(8,128)} %param.9, f32[1024,256]{1,0:T(8,128)S(1)} %copy-done.1, f32[1024]{0:T(1024)S(1)} %copy-done.11), kind=kOutput, calls=%fused_computation.7 | convolution fusion | flops 1611399168 | bytes 7344128 | tf_op jit(solution)/shard_map/dot_general | solution.py:432
  79.5 1.8 fusion.14
  81.3 1.8 convolution_bitcast_fusion.3
  83.2 0.9 pad_maximum_fusion.g
  84.1 46.6 %sum_all_768.1.grams = f32[768,256]{1,0:T(8,128)} custom-call(f32[768,256]{1,0:T(8,128)} %pad_maximum_fusion.g), custom_call_target="tpu_custom_call" | custom-call | tf_op jit(solution)/shard_map/sum_all_768/pallas_call | solution.py:324
  130.7 32.6 %first_steps.1 = (f32[256,256]{1,0:T(8,128)}, f32[256,256]{1,0:T(8,128)}) custom-call(f32[768,256]{1,0:T(8,128)} %sum_all_768.1.grams), custom_call_target="tpu_custom_call" | custom-call | tf_op jit(solution)/shard_map/first_steps/pallas_call | solution.py:407
  163.3 2.0 convolution_subtract_fusion.1
  165.3 1.8 fusion.18
  167.2 1.2 fusion.4
  168.4 1.8 fusion.15.coef
  170.2 66.2 %far_exchange.3 = f32[256,512]{1,0:T(8,128)} custom-call(s32[4,8]{1,0:T(4,128)} %pad_add_fusion.meta, f32[256,512]{1,0:T(8,128)} %fusion.15.coef, f32[6,512,512]{2,1,0:T(8,128)} %c_hbm.3), custom_call_target="tpu_custom_call" | custom-call | tf_op jit(solution)/shard_map/far_exchange/pallas_call | solution.py:231
  236.4 2.1 fusion.16
  238.5 4.0 %fusion.1 = f32[1024,256]{1,0:T(8,128)S(1)} fusion(f32[256,1024]{0,1:T(8,128)S(1)} %fusion.16, f32[1024,256]{1,0:T(8,128)S(1)} %fusion.4, f32[1024,1024]{1,0:T(8,128)} %param.9, f32[1024]{0:T(1024)S(1)} %copy-done.11), kind=kOutput, calls=%fused_computation.3 | convolution fusion | flops 1611399168 | bytes 7344128 | tf_op jit(solution)/shard_map/dot_general | solution.py:432
  242.6 1.8 fusion.17
  244.4 0.8 pad_maximum_fusion.1.g
  245.3 38.6 %sum_all_512.1 = f32[512,256]{1,0:T(8,128)} custom-call(f32[512,256]{1,0:T(8,128)} %pad_maximum_fusion.1.g), custom_call_target="tpu_custom_call" | custom-call | tf_op jit(solution)/shard_map/sum_all_512/pallas_call | solution.py:324
  283.9 1.7 slice.7
  285.6 1.1 copy.30
  286.7 2.0 fusion.5
  288.8 25.4 %second_step.1 = f32[256,256]{1,0:T(8,128)} custom-call(f32[256,256]{1,0:T(8,128)} %get-tuple-element.13.curv, f32[256,256]{1,0:T(8,128)} %get-tuple-element.12.cur), custom_call_target="tpu_custom_call" | custom-call | tf_op jit(solution)/shard_map/second_step/pallas_call | solution.py:407
  314.1 3.0 convolution_subtract_fusion
  317.1 1.1 fusion.19
  318.2 2.8 fusion.3
  321.0 2.5 copy.24
  (28 shorter events, 0.2 us)
Async XLA Ops:
  0.6 7.0 %copy-start = (f32[1024,512]{1,0:T(8,128)S(1)}, f32[1024,512]{1,0:T(8,128)}, u32[]{:S(2)}) copy-start(f32[1024,512]{1,0:T(8,128)} %param.10) | copy-start | bytes 6291460
  0.6 7.0 %copy-start.1 = (f32[1024,256]{1,0:T(8,128)S(1)}, f32[1024,256]{1,0:T(8,128)}, u32[]{:S(2)}) copy-start(f32[1024,256]{1,0:T(8,128)} %param.7) | copy-start | bytes 3145732
  73.3 2.1 copy-start.11
  163.3 3.9 %copy-start.10 = (f32[256,256]{1,0:T(8,128)S(1)}, f32[256,256]{1,0:T(8,128)}, u32[]{:S(2)}) copy-start(f32[256,256]{1,0:T(8,128)} %get-tuple-element.7) | copy-start | bytes 786436
  165.3 1.9 copy-start.2
  168.4 74.2 %copy-start.4 = (f32[1024,256]{1,0:T(8,128)}, f32[1024,256]{1,0:T(8,128)S(1)}, u32[]{:S(2)}) copy-start(f32[1024,256]{1,0:T(8,128)S(1)} %fusion.4) | copy-start | bytes 3145732
  242.6 1.9 copy-start.6
  286.7 27.4 %copy-start.3 = (f32[1024,256]{1,0:T(8,128)S(1)}, f32[1024,256]{1,0:T(8,128)}, u32[]{:S(2)}) copy-start(f32[1024,256]{1,0:T(8,128)} %copy-done.2) | copy-start | bytes 3145732
  286.7 27.4 %copy-start.7 = (f32[1024,256]{1,0:T(8,128)S(1)}, f32[1024,256]{1,0:T(8,128)}, u32[]{:S(2)}) copy-start(f32[1024,256]{1,0:T(8,128)} %copy-done.6) | copy-start | bytes 3145732
  288.7 28.3 %copy-start.5 = (f32[1024,256]{1,0:T(8,128)S(1)}, f32[1024,256]{1,0:T(8,128)}, u32[]{:S(2)}) copy-start(f32[1024,256]{1,0:T(8,128)} %copy-done.4) | copy-start | bytes 3145732
  314.1 3.0 copy-start.8
  314.1 4.1 %copy-start.9 = (f32[256,256]{1,0:T(8,128)S(1)}, f32[256,256]{1,0:T(8,128)}, u32[]{:S(2)}) copy-start(f32[256,256]{1,0:T(8,128)} %get-tuple-element.6) | copy-start | bytes 786436
where the time goes:
time: 329 us; the launch traced here: 324 us
  Pallas kernels  273 us (83%)
  matrix products  36.7 us (11%)
  other arithmetic  6.61 us (2%)
  local copies, waits for them, and re-layouts  5.34 us (2%)
    pallas_call x2, Pallas kernels, far_exchange(): pl.pallas_call(functools.partial(far_kernel, n), out_shape=jax.ShapeDtype...  130 us
    pallas_call x2, Pallas kernels, sum_all(): pl.pallas_call(functools.partial(sum_kernel, n), out_shape=jax.ShapeDtype...  85.3 us
    pallas_call x2, Pallas kernels, local_call(): pl.pallas_call(kernel, out_shape=out_shapes, compiler_params=pltpu.Compil...  57.9 us
    dot_general x5, matrix products, gram(): return lax.dot_general(x, y, contract_first, precision=highest)  10.7 us
    dot_general x2, matrix products, image_of(): near = jnp.dot(near_block, vectors, precision=high)  8.08 us

commit v1 on v0

--- a/solution.py
+++ b/solution.py
@@ -351,15 +351,24 @@
     lane = lax.broadcasted_iota(jnp.int32, (1, size), 1)
     sub = lax.broadcasted_iota(jnp.int32, (size, 1), 0)
     mats = list(mats)
-    for step in range(size):
+    for k0 in range(0, size, 2):
+        k1 = k0 + 1
+        at_lane = jnp.logical_or(lane == k0, lane == k1)
+        at_sub = jnp.logical_or(sub == k0, sub == k1)
         for m, mat in enumerate(mats):
-            row = mat[step:step + 1, :]
-            col = mat[:, step:step + 1]
-            inv = 1.0 / mat[step:step + 1, step:step + 1]
-            scaled = jnp.where(lane == step, inv, row * inv)
-            factor = jnp.where(sub == step, -1.0, col)
-            kept = jnp.where(jnp.logical_or(lane == step, sub == step), 0.0, mat)
-            mats[m] = kept - factor * scaled
+            row0, row1 = mat[k0:k1, :], mat[k1:k1 + 1, :]
+            col0, col1 = mat[:, k0:k1], mat[:, k1:k1 + 1]
+            p00, p01 = row0[:, k0:k1], row0[:, k1:k1 + 1]
+            p10, p11 = row1[:, k0:k1], row1[:, k1:k1 + 1]
+            inv = 1.0 / (p00 * p11 - p01 * p10)
+            unit0 = jnp.where(lane == k0, 1.0, jnp.where(lane == k1, 0.0, row0))
+            unit1 = jnp.where(lane == k1, 1.0, jnp.where(lane == k0, 0.0, row1))
+            scaled0 = (p11 * unit0 - p01 * unit1) * inv
+            scaled1 = (p00 * unit1 - p10 * unit0) * inv
+            factor0 = jnp.where(sub == k0, -1.0, jnp.where(sub == k1, 0.0, col0))
+            factor1 = jnp.where(sub == k1, -1.0, jnp.where(sub == k0, 0.0, col1))
+            kept = jnp.where(jnp.logical_or(at_lane, at_sub), 0.0, mat)
+            mats[m] = (kept - factor0 * scaled0) - factor1 * scaled1
     return mats
 
 
@@ -384,7 +393,7 @@
     return 0.5 * (matrix + jnp.transpose(matrix))
 
 
-def first_kernel(grams, alpha_ref, beta_ref):
+def first_kernel(grams, alpha_ref, beta_ref, updated_ref):
     size = grams.shape[1]
     g0 = symmetric(grams[:size, :])
     g1 = symmetric(grams[size:2 * size, :])
@@ -395,6 +404,7 @@
     inner = mm(g2, alpha) - g1
     cross = mm(g1, alpha)
     updated = symmetric((g0 - cross) + mm(alpha, inner, contract_first))
+    updated_ref[...] = updated
     beta_ref[...] = mm(i0, updated)
 
 
@@ -441,13 +451,12 @@
     local = jnp.concatenate([
         gram(right_sides, right_sides), gram(right_sides, image), gram(image, image)])
     grams = sum_all(n, local, 1)
-    alpha, beta = local_call(first_kernel, (square, square), "first_steps", grams)
+    alpha, beta, updated = local_call(first_kernel, (square,) * 3, "first_steps", grams)
     residual = right_sides - jnp.dot(image, alpha, precision=highest)
     direction = residual + jnp.dot(right_sides, beta, precision=highest)
     image2 = image_of(direction)
-    both = jnp.concatenate([gram(direction, image2), gram(residual, residual)])
-    summed = sum_all(n, both, 2)
-    alpha2 = local_call(second_kernel, square, "second_step", summed[:cols], symmetric(summed[cols:]))
+    curvature = sum_all(n, gram(direction, image2), 2)
+    alpha2 = local_call(second_kernel, square, "second_step", curvature, updated)
     answer = jnp.dot(right_sides, alpha, precision=highest) + jnp.dot(direction, alpha2, precision=highest)
     residual = residual - jnp.dot(image2, alpha2, precision=highest)
     return answer, residual

time: 329 us -> 330 us (level)
  Pallas kernels: 273 us -> 282 us
    pallas_call x2, Pallas kernels: 57.9 us -> 74.5 us  [local_call(): pl.pallas_call(kernel, out_shape=out_shapes, compiler_params=pltpu.Compil...]
    pallas_call x2, Pallas kernels: 85.3 us -> 77.2 us  [sum_all(): pl.pallas_call(functools.partial(sum_kernel, n), out_shape=jax.ShapeDtype...]
    dot_general x5 -> x4, matrix products: 10.7 us -> 9.58 us  [gram(): return lax.dot_general(x, y, contract_first, precision=highest)]
where the time goes in v1:
time: 330 us; the launch traced here: 325 us
  Pallas kernels  282 us (85%)
  matrix products  35.4 us (11%)
  other arithmetic  3.75 us (1%)
    pallas_call x2, Pallas kernels, far_exchange(): pl.pallas_call(functools.partial(far_kernel, n), out_shape=jax.ShapeDtype...  130 us
    pallas_call x2, Pallas kernels, sum_all(): pl.pallas_call(functools.partial(sum_kernel, n), out_shape=jax.ShapeDtype...  77.2 us
    pallas_call x2, Pallas kernels, local_call(): pl.pallas_call(kernel, out_shape=out_shapes, compiler_params=pltpu.Compil...  74.5 us
    dot_general x4, matrix products, gram(): return lax.dot_general(x, y, contract_first, precision=highest)  9.58 us
    dot_general x2, matrix products, image_of(): near = jnp.dot(near_block, vectors, precision=high)  8.07 us

profile of v1, /device:TPU:0, one launch (start us, length us, event | category | flops | bytes accessed | tf_op | source)
XLA Modules:
  0.0 325.3 jit_solution(11572475416668843907)
XLA Ops:
  0.6 0.0 copy-start
  0.6 0.0 copy-start.1
  1.5 0.8 fusion.7
  2.3 0.1 fusion.6
  2.4 0.7 and_select_fusion
  3.1 0.6 iota_reduce_fusion
  3.7 0.6 pad_add_fusion.meta
  4.3 3.4 %fusion.11 = f32[256,256]{1,0:T(8,128)S(1)} fusion(f32[1024,256]{1,0:T(8,128)} %param.7), kind=kOutput, calls=%fused_computation.33 | convolution fusion | flops 805306368 | bytes 1310720 | tf_op jit(solution)/shard_map/dot_general | solution.py:448
  7.7 1.8 fusion.12.coef
  9.5 63.8 %far_exchange.2 = f32[256,512]{1,0:T(8,128)} custom-call(s32[4,8]{1,0:T(4,128)} %pad_add_fusion.meta, f32[256,512]{1,0:T(8,128)} %fusion.12.coef, f32[6,512,512]{2,1,0:T(8,128)} %c_hbm.3), custom_call_target="tpu_custom_call" | custom-call | tf_op jit(solution)/shard_map/far_exchange/pallas_call | solution.py:231
  73.4 0.0 copy-start.5
  73.4 2.1 convolution_bitcast_fusion
  75.5 4.0 %fusion.2 = f32[1024,256]{1,0:T(8,128)S(1)} fusion(f32[1024,256]{1,0:T(8,128)S(1)} %convolution_bitcast_fusion, f32[1024,1024]{1,0:T(8,128)} %param.9, f32[1024,256]{1,0:T(8,128)S(1)} %copy-done.1, f32[1024]{0:T(1024)S(1)} %copy-done.5), kind=kOutput, calls=%fused_computation.7 | convolution fusion | flops 1611399168 | bytes 7344128 | tf_op jit(solution)/shard_map/dot_general | solution.py:442
  79.5 1.8 fusion.13
  81.4 1.8 convolution_bitcast_fusion.3
  83.2 0.9 pad_maximum_fusion.g
  84.1 46.6 %sum_all_768.1.grams = f32[768,256]{1,0:T(8,128)} custom-call(f32[768,256]{1,0:T(8,128)} %pad_maximum_fusion.g), custom_call_target="tpu_custom_call" | custom-call | tf_op jit(solution)/shard_map/sum_all_768/pallas_call | solution.py:324
  130.8 41.3 %first_steps.1 = (f32[256,256]{1,0:T(8,128)}, f32[256,256]{1,0:T(8,128)}, f32[256,256]{1,0:T(8,128)}) custom-call(f32[768,256]{1,0:T(8,128)} %sum_all_768.1.grams), custom_call_target="tpu_custom_call" | custom-call | tf_op jit(solution)/shard_map/first_steps/pallas_call | solution.py:417
  172.1 2.0 convolution_subtract_fusion.1
  174.1 0.0 copy-done.4
  174.1 1.0 fusion.4
  175.1 1.8 fusion.14.coef
  176.9 66.2 %far_exchange.3 = f32[256,512]{1,0:T(8,128)} custom-call(s32[4,8]{1,0:T(4,128)} %pad_add_fusion.meta, f32[256,512]{1,0:T(8,128)} %fusion.14.coef, f32[6,512,512]{2,1,0:T(8,128)} %c_hbm.3), custom_call_target="tpu_custom_call" | custom-call | tf_op jit(solution)/shard_map/far_exchange/pallas_call | solution.py:231
  243.1 2.1 fusion.15
  245.2 4.0 %fusion.1 = f32[1024,256]{1,0:T(8,128)S(1)} fusion(f32[256,1024]{0,1:T(8,128)S(1)} %fusion.15, f32[1024,256]{1,0:T(8,128)S(1)} %fusion.4, f32[1024,1024]{1,0:T(8,128)} %param.9, f32[1024]{0:T(1024)S(1)} %copy-done.5), kind=kOutput, calls=%fused_computation.3 | convolution fusion | flops 1611399168 | bytes 7344128 | tf_op jit(solution)/shard_map/dot_general | solution.py:442
  249.3 2.5 fusion.16.g
  251.8 30.5 %sum_all_256.1.curv = f32[256,256]{1,0:T(8,128)} custom-call(f32[256,256]{1,0:T(8,128)} %fusion.16.g), custom_call_target="tpu_custom_call" | custom-call | tf_op jit(solution)/shard_map/sum_all_256/pallas_call | solution.py:324
  282.3 33.3 %second_step.1 = f32[256,256]{1,0:T(8,128)} custom-call(f32[256,256]{1,0:T(8,128)} %sum_all_256.1.curv, f32[256,256]{1,0:T(8,128)} %get-tuple-element.9.cur), custom_call_target="tpu_custom_call" | custom-call | tf_op jit(solution)/shard_map/second_step/pallas_call | solution.py:417
  315.6 3.0 convolution_subtract_fusion
  318.6 1.1 fusion.17
  319.7 2.8 fusion.3
  322.5 2.5 copy.20
  (11 shorter events, 0.0 us)
Async XLA Ops:
  0.6 7.1 %copy-start = (f32[1024,512]{1,0:T(8,128)S(1)}, f32[1024,512]{1,0:T(8,128)}, u32[]{:S(2)}) copy-start(f32[1024,512]{1,0:T(8,128)} %param.10) | copy-start | bytes 6291460
  0.6 7.1 %copy-start.1 = (f32[1024,256]{1,0:T(8,128)S(1)}, f32[1024,256]{1,0:T(8,128)}, u32[]{:S(2)}) copy-start(f32[1024,256]{1,0:T(8,128)} %param.7) | copy-start | bytes 3145732
  73.4 2.1 copy-start.5
  172.1 2.0 copy-start.4
  315.6 3.0 copy-start.2
  315.6 4.1 %copy-start.3 = (f32[256,256]{1,0:T(8,128)S(1)}, f32[256,256]{1,0:T(8,128)}, u32[]{:S(2)}) copy-start(f32[256,256]{1,0:T(8,128)} %get-tuple-element.7) | copy-start | bytes 786436

commit v2 on v0

--- a/solution.py
+++ b/solution.py
@@ -32,8 +32,14 @@
     return d(a_hi, b_hi) + (d(a_hi, b_lo) + d(a_lo, b_hi))
 
 
-def far_kernel(n, meta, coef, c_hbm, out, cv, ahead, ret, rs, ri, up, rz,
-               c_sem, fs, fr, ss, sr, xs, xr, zs, zr):
+def far_kernel(n, solve, *refs):
+    if solve:
+        meta, coef, c_hbm, grams, out, alpha, beta, updated = refs[:8]
+        refs = refs[8:]
+    else:
+        meta, coef, c_hbm, out = refs[:4]
+        refs = refs[4:]
+    cv, ahead, ret, rs, ri, up, rz, c_sem, fs, fr, ss, sr, xs, xr, zs, zr = refs[:16]
     me = lax.axis_index("clu")
     z = me // GROUP
     p = me % GROUP
@@ -69,20 +75,23 @@
             return c
         lax.fori_loop(0, GROUP, zero, 0)
 
-    barrier = pltpu.get_barrier_semaphore()
-    pl.semaphore_signal(barrier, inc=1, device_id=(sib,), device_id_type=MESH)
-    for i in (1, 2, 3):
-        pl.semaphore_signal(barrier, inc=1, device_id=(base + chips[i] * 2 + k,), device_id_type=MESH)
-
-    @pl.when(has_up)
-    def _():
-        pl.semaphore_signal(barrier, inc=1, device_id=(me + GROUP,), device_id_type=MESH)
-
-    @pl.when(has_down)
-    def _():
-        pl.semaphore_signal(barrier, inc=1, device_id=(me - GROUP,), device_id_type=MESH)
-
-    pl.semaphore_wait(barrier, 4 + jnp.where(has_up, 1, 0) + jnp.where(has_down, 1, 0))
+    if solve:
+        greet_all(n, me)
+    else:
+        barrier = pltpu.get_barrier_semaphore()
+        pl.semaphore_signal(barrier, inc=1, device_id=(sib,), device_id_type=MESH)
+        for i in (1, 2, 3):
+            pl.semaphore_signal(barrier, inc=1, device_id=(base + chips[i] * 2 + k,), device_id_type=MESH)
+
+        @pl.when(has_up)
+        def _():
+            pl.semaphore_signal(barrier, inc=1, device_id=(me + GROUP,), device_id_type=MESH)
+
+        @pl.when(has_down)
+        def _():
+            pl.semaphore_signal(barrier, inc=1, device_id=(me - GROUP,), device_id_type=MESH)
+
+        pl.semaphore_wait(barrier, 4 + jnp.where(has_up, 1, 0) + jnp.where(has_down, 1, 0))
 
     f_z = rc(coef, ahead.at[p], fs.at[0], fr.at[0], me - GROUP)
 
@@ -120,6 +129,10 @@
     @pl.when(k == 1)
     def _():
         f_s_own.start()
+
+    if solve:
+        total = refs[16]
+        finish_sum, drain_sum = start_sum(n, me, grams, total, *refs[17:])
 
     c_copy.wait()
 
@@ -158,6 +171,10 @@
         t = chips[i] * 2 + k
         ret[t] = ret[t] + rs[i]
         r_x[i].start()
+
+    if solve:
+        finish_sum()
+        first_kernel(total, alpha, beta, updated)
 
     for i in (1, 2, 3):
         @pl.when(jnp.logical_or(chips[i] > a, has_up))
@@ -224,19 +241,29 @@
     def _():
         r_z.wait_send()
 
-
-def far_exchange(n, meta, coef_t, couplings):
+    if solve:
+        drain_sum()
+
+
+def far_exchange(n, meta, coef_t, couplings, grams=None):
     blk = coef_t.shape
     f32 = jnp.float32
+    solve = grams is not None
+    vmem = pl.BlockSpec(memory_space=pltpu.VMEM)
+    one = jax.ShapeDtypeStruct(blk, f32)
+    extra = []
+    if solve:
+        square = jax.ShapeDtypeStruct((grams.shape[1],) * 2, f32)
+        extra = [pltpu.VMEM(grams.shape, f32)] + sum_scratch(n, grams)
     return pl.pallas_call(
-        functools.partial(far_kernel, n),
-        out_shape=jax.ShapeDtypeStruct(blk, f32),
+        functools.partial(far_kernel, n, solve),
+        out_shape=(one, square, square, square) if solve else one,
         in_specs=[
             pl.BlockSpec(memory_space=pltpu.SMEM),
             pl.BlockSpec(memory_space=pltpu.VMEM),
             pl.BlockSpec(memory_space=pl.ANY),
-        ],
-        out_specs=pl.BlockSpec(memory_space=pltpu.VMEM),
+        ] + [vmem] * solve,
+        out_specs=(vmem,) * 4 if solve else vmem,
         scratch_shapes=[
             pltpu.VMEM(couplings.shape, f32),
             pltpu.VMEM((GROUP,) + blk, f32),
@@ -254,21 +281,15 @@
             pltpu.SemaphoreType.DMA((3,)),
             pltpu.SemaphoreType.DMA,
             pltpu.SemaphoreType.DMA,
-        ],
+        ] + extra,
         compiler_params=pltpu.CompilerParams(
-            collective_id=0, has_side_effects=True, vmem_limit_bytes=VMEM_LIMIT),
-        name="far_exchange",
-    )(meta, coef_t, couplings)
-
-
-def sum_kernel(n, g, out, inbox, planes, s1, r1, s2, r2, s3, r3):
-    me = lax.axis_index("clu")
-    z = me // GROUP
-    p = me % GROUP
-    base = z * GROUP
-    groups = n // GROUP
-    rows = g.shape[0] // GROUP
-
+            collective_id=int(solve), has_side_effects=True, vmem_limit_bytes=VMEM_LIMIT),
+        name="far_exchange_solve" if solve else "far_exchange",
+    )(meta, coef_t, couplings, *([grams] if solve else []))
+
+
+def greet_all(n, me):
+    base, p, groups = me // GROUP * GROUP, me % GROUP, n // GROUP
     barrier = pltpu.get_barrier_semaphore()
     for j in range(1, GROUP):
         pl.semaphore_signal(barrier, inc=1, device_id=(base + (p + j) % GROUP,), device_id_type=MESH)
@@ -276,6 +297,15 @@
         pl.semaphore_signal(barrier, inc=1, device_id=((me + j * GROUP) % n,), device_id_type=MESH)
     pl.semaphore_wait(barrier, GROUP - 1 + groups - 1)
 
+
+def start_sum(n, me, g, out, inbox, planes, s1, r1, s2, r2, s3, r3):
+    z = me // GROUP
+    p = me % GROUP
+    base = z * GROUP
+    groups = n // GROUP
+    rows = g.shape[0] // GROUP
+    pending = []
+
     def rc(src, dst, ssem, rsem, dev):
         return pltpu.make_async_remote_copy(
             src_ref=src, dst_ref=dst, send_sem=ssem, recv_sem=rsem,
@@ -284,58 +314,68 @@
     def part(t):
         return pl.ds(pl.multiple_of(t * rows, 8), rows)
 
-    scatter = []
     for j in range(1, GROUP):
         t = (p + j) % GROUP
-        scatter.append(rc(g.at[part(t)], inbox.at[j - 1], s1.at[j - 1], r1.at[j - 1], base + t))
-        scatter[-1].start()
-    total = g[part(p), :]
-    for j in range(1, GROUP):
-        scatter[j - 1].wait_recv()
-        total = total + inbox[j - 1]
-    planes[z] = total
-    across = []
-    for j in range(1, groups):
-        across.append(rc(planes.at[z], planes.at[z], s2.at[j - 1], r2.at[j - 1], (me + j * GROUP) % n))
-        across[-1].start()
-    for j in range(1, groups):
-        src = (z + groups - j) % groups
-        rc(planes.at[src], planes.at[src], s2.at[j - 1], r2.at[j - 1], (me + j * GROUP) % n).wait_recv()
-    total = planes[0]
-    for j in range(1, groups):
-        total = total + planes[j]
-    out[part(p), :] = total
-    gather = []
-    for j in range(1, GROUP):
-        t = (p + j) % GROUP
-        gather.append(rc(out.at[part(p)], out.at[part(p)], s3.at[j - 1], r3.at[j - 1], base + t))
-        gather[-1].start()
-    for j in range(1, GROUP):
-        t = (p + GROUP - j) % GROUP
-        rc(out.at[part(t)], out.at[part(t)], s3.at[j - 1], r3.at[j - 1], base + t).wait_recv()
-    for copy in scatter + across + gather:
-        copy.wait_send()
+        pending.append(rc(g.at[part(t)], inbox.at[j - 1], s1.at[j - 1], r1.at[j - 1], base + t))
+        pending[-1].start()
+    scatter = list(pending)
+
+    def finish():
+        total = g[part(p), :]
+        for j in range(1, GROUP):
+            scatter[j - 1].wait_recv()
+            total = total + inbox[j - 1]
+        planes[z] = total
+        for j in range(1, groups):
+            pending.append(rc(planes.at[z], planes.at[z], s2.at[j - 1], r2.at[j - 1], (me + j * GROUP) % n))
+            pending[-1].start()
+        for j in range(1, groups):
+            src = (z + groups - j) % groups
+            rc(planes.at[src], planes.at[src], s2.at[j - 1], r2.at[j - 1], (me + j * GROUP) % n).wait_recv()
+        total = planes[0]
+        for j in range(1, groups):
+            total = total + planes[j]
+        out[part(p), :] = total
+        for j in range(1, GROUP):
+            t = (p + j) % GROUP
+            pending.append(rc(out.at[part(p)], out.at[part(p)], s3.at[j - 1], r3.at[j - 1], base + t))
+            pending[-1].start()
+        for j in range(1, GROUP):
+            t = (p + GROUP - j) % GROUP
+            rc(out.at[part(t)], out.at[part(t)], s3.at[j - 1], r3.at[j - 1], base + t).wait_recv()
+
+    def drain():
+        for copy in pending:
+            copy.wait_send()
+
+    return finish, drain
+
+
+def sum_kernel(n, g, out, *refs):
+    me = lax.axis_index("clu")
+    greet_all(n, me)
+    finish, drain = start_sum(n, me, g, out, *refs)
+    finish()
+    drain()
+
+
+def sum_scratch(n, g):
+    rows, groups = g.shape[0] // GROUP, n // GROUP
+    counts = (GROUP - 1, GROUP - 1, groups - 1, groups - 1, GROUP - 1, GROUP - 1)
+    return [
+        pltpu.VMEM((GROUP - 1, rows, g.shape[1]), jnp.float32),
+        pltpu.VMEM((groups, rows, g.shape[1]), jnp.float32),
+    ] + [pltpu.SemaphoreType.DMA((c,)) for c in counts]
 
 
 def sum_all(n, g, collective_id):
-    rows = g.shape[0] // GROUP
-    groups = n // GROUP
     f32 = jnp.float32
     return pl.pallas_call(
         functools.partial(sum_kernel, n),
         out_shape=jax.ShapeDtypeStruct(g.shape, f32),
         in_specs=[pl.BlockSpec(memory_space=pltpu.VMEM)],
         out_specs=pl.BlockSpec(memory_space=pltpu.VMEM),
-        scratch_shapes=[
-            pltpu.VMEM((GROUP - 1, rows, g.shape[1]), f32),
-            pltpu.VMEM((groups, rows, g.shape[1]), f32),
-            pltpu.SemaphoreType.DMA((GROUP - 1,)),
-            pltpu.SemaphoreType.DMA((GROUP - 1,)),
-            pltpu.SemaphoreType.DMA((groups - 1,)),
-            pltpu.SemaphoreType.DMA((groups - 1,)),
-            pltpu.SemaphoreType.DMA((GROUP - 1,)),
-            pltpu.SemaphoreType.DMA((GROUP - 1,)),
-        ],
+        scratch_shapes=sum_scratch(n, g),
         compiler_params=pltpu.CompilerParams(
             collective_id=collective_id, has_side_effects=True, vmem_limit_bytes=VMEM_LIMIT),
         name="sum_all_%d" % g.shape[0],
@@ -350,17 +390,23 @@
     size = mats[0].shape[0]
     lane = lax.broadcasted_iota(jnp.int32, (1, size), 1)
     sub = lax.broadcasted_iota(jnp.int32, (size, 1), 0)
-    mats = list(mats)
-    for step in range(size):
-        for m, mat in enumerate(mats):
-            row = mat[step:step + 1, :]
-            col = mat[:, step:step + 1]
-            inv = 1.0 / mat[step:step + 1, step:step + 1]
-            scaled = jnp.where(lane == step, inv, row * inv)
-            factor = jnp.where(sub == step, -1.0, col)
-            kept = jnp.where(jnp.logical_or(lane == step, sub == step), 0.0, mat)
-            mats[m] = kept - factor * scaled
-    return mats
+    unroll = 8
+
+    def body(_, state):
+        state = list(state)
+        for step in range(unroll):
+            for m, mat in enumerate(state):
+                row = mat[step:step + 1, :]
+                col = mat[:, step:step + 1]
+                inv = 1.0 / mat[step:step + 1, step:step + 1]
+                scaled = jnp.where(lane == step, inv, row * inv)
+                factor = jnp.where(sub == step, -1.0, col)
+                kept = jnp.where(jnp.logical_or(lane == step, sub == step), 0.0, mat)
+                state[m] = kept - factor * scaled
+        state = [jnp.concatenate([x[unroll:], x[:unroll]], axis=0) for x in state]
+        return tuple(pltpu.roll(x, size - unroll, 1) for x in state)
+
+    return list(lax.fori_loop(0, size // unroll, body, tuple(mats)))
 
 
 def invert(mats):
@@ -384,7 +430,7 @@
     return 0.5 * (matrix + jnp.transpose(matrix))
 
 
-def first_kernel(grams, alpha_ref, beta_ref):
+def first_kernel(grams, alpha_ref, beta_ref, updated_ref):
     size = grams.shape[1]
     g0 = symmetric(grams[:size, :])
     g1 = symmetric(grams[size:2 * size, :])
@@ -395,6 +441,7 @@
     inner = mm(g2, alpha) - g1
     cross = mm(g1, alpha)
     updated = symmetric((g0 - cross) + mm(alpha, inner, contract_first))
+    updated_ref[...] = updated
     beta_ref[...] = mm(i0, updated)
 
 
@@ -427,27 +474,28 @@
         jnp.pad(live.astype(jnp.int32), pad),
     ])
 
-    def image_of(vectors):
-        coef_t = lax.dot_general(vectors, cluster_basis, contract_first, precision=high)
+    def coefficients(vectors):
+        return lax.dot_general(vectors, cluster_basis, contract_first, precision=high)
+
+    def image_of(vectors, far_t):
         near = jnp.dot(near_block, vectors, precision=high)
-        far_t = far_exchange(n, meta, coef_t, couplings)
         far = lax.dot_general(cluster_basis, far_t, contract_last, precision=high)
         return diag_shift[:, None] * vectors + (near + far)
 
     def gram(x, y):
         return lax.dot_general(x, y, contract_first, precision=highest)
 
-    image = image_of(right_sides)
+    far_b = far_exchange(n, meta, coefficients(right_sides), couplings)
+    image = image_of(right_sides, far_b)
     local = jnp.concatenate([
         gram(right_sides, right_sides), gram(right_sides, image), gram(image, image)])
-    grams = sum_all(n, local, 1)
-    alpha, beta = local_call(first_kernel, (square, square), "first_steps", grams)
+    far_w, alpha, beta, updated = far_exchange(n, meta, coefficients(image), couplings, local)
     residual = right_sides - jnp.dot(image, alpha, precision=highest)
     direction = residual + jnp.dot(right_sides, beta, precision=highest)
-    image2 = image_of(direction)
-    both = jnp.concatenate([gram(direction, image2), gram(residual, residual)])
-    summed = sum_all(n, both, 2)
-    alpha2 = local_call(second_kernel, square, "second_step", summed[:cols], symmetric(summed[cols:]))
+    far_d = far_b + (gram(beta, far_b) - gram(alpha, far_w))
+    image2 = image_of(direction, far_d)
+    curvature = sum_all(n, gram(direction, image2), 2)
+    alpha2 = local_call(second_kernel, square, "second_step", curvature, updated)
     answer = jnp.dot(right_sides, alpha, precision=highest) + jnp.dot(direction, alpha2, precision=highest)
     residual = residual - jnp.dot(image2, alpha2, precision=highest)
     return answer, residual

time: 329 us -> 283 us (0.86); the launches traced: 324 us -> 283 us
  Pallas kernels: 273 us -> 241 us
    pallas_call x2 -> x1, Pallas kernels: 85.3 us -> 27.4 us  [sum_all(): pl.pallas_call(functools.partial(sum_kernel, n), out_shape=jax.ShapeDtype...]
    pallas_call x2, Pallas kernels: 130 us -> 186 us  [far_exchange(): pl.pallas_call(functools.partial(far_kernel, n, solve), out_shape=(one, s...]
    pallas_call x2 -> x1, Pallas kernels: 57.9 us -> 27.4 us  [local_call(): pl.pallas_call(kernel, out_shape=out_shapes, compiler_params=pltpu.Compil...]
    dot_general x5 -> x6, matrix products: 10.7 us -> 11.1 us  [gram(): return lax.dot_general(x, y, contract_first, precision=highest)]
where the time goes in v2:
time: 283 us
  Pallas kernels  241 us (85%)
  matrix products  33.8 us (12%)
  other arithmetic  3.76 us (1%)
    pallas_call x2, Pallas kernels, far_exchange(): pl.pallas_call(functools.partial(far_kernel, n, solve), out_shape=(one, s...  186 us
    pallas_call x1, Pallas kernels, sum_all(): pl.pallas_call(functools.partial(sum_kernel, n), out_shape=jax.ShapeDtype...  27.4 us
    pallas_call x1, Pallas kernels, local_call(): pl.pallas_call(kernel, out_shape=out_shapes, compiler_params=pltpu.Compil...  27.4 us
    dot_general x6, matrix products, gram(): return lax.dot_general(x, y, contract_first, precision=highest)  11.1 us
    dot_general x2, matrix products, image_of(): near = jnp.dot(near_block, vectors, precision=high)  5.94 us

profile of v2, /device:TPU:0, one launch (start us, length us, event | category | flops | bytes accessed | tf_op | source)
XLA Modules:
  0.0 282.6 jit_solution(2464834433032291184)
XLA Ops:
  0.6 0.0 copy-start
  0.6 0.0 copy-start.1
  1.5 0.8 fusion.8
  2.3 0.1 fusion.7
  2.4 0.7 and_select_fusion
  3.1 0.6 iota_reduce_fusion
  3.7 0.6 pad_add_fusion.refs_0_
  4.3 3.6 %fusion.14 = f32[256,256]{1,0:T(8,128)S(1)} fusion(f32[1024,256]{1,0:T(8,128)} %param.7), kind=kOutput, calls=%fused_computation.37 | convolution fusion | flops 805306368 | bytes 1310720 | tf_op jit(solution)/shard_map/dot_general | solution.py:486
  8.0 1.8 fusion.12.refs_1_
  9.8 63.8 %far_exchange.1 = f32[256,512]{1,0:T(8,128)} custom-call(s32[4,8]{1,0:T(4,128)} %pad_add_fusion.refs_0_, f32[256,512]{1,0:T(8,128)} %fusion.12.refs_1_, f32[6,512,512]{2,1,0:T(8,128)} %refs_2_.3), custom_call_target="tpu_custom_call" | custom-call | tf_op jit(solution)/shard_map/far_exchange/pallas_call | solution.py:258
  73.6 0.0 copy-start.8
  73.6 2.1 convolution_bitcast_fusion
  75.7 4.0 %fusion.2 = f32[1024,256]{1,0:T(8,128)S(1)} fusion(f32[1024,256]{1,0:T(8,128)S(1)} %convolution_bitcast_fusion, f32[1024,1024]{1,0:T(8,128)} %param.9, f32[1024,256]{1,0:T(8,128)S(1)} %copy-done.1, f32[1024]{0:T(1024)S(1)} %copy-done.8), kind=kOutput, calls=%fused_computation.7 | convolution fusion | flops 1611399168 | bytes 7344128 | tf_op jit(solution)/shard_map/dot_general | solution.py:481
  79.8 1.8 fusion.15
  81.6 1.8 convolution_bitcast_fusion.3
  83.5 0.9 pad_maximum_fusion.refs_3_
  84.4 1.8 fusion.13.refs_1_
  86.2 122.1 %far_exchange_solve.1 = (f32[256,512]{1,0:T(8,128)}, f32[256,256]{1,0:T(8,128)}, f32[256,256]{1,0:T(8,128)}, f32[256,256]{1,0:T(8,128)}) custom-call(s32[4,8]{1,0:T(4,128)} %pad_add_fusion.refs_0_, f32[256,512]{1,0:T(8,128)} %fusion.13.refs_1_, f32[6,512,512]{2,1,0:T(8,128)} %refs_2_.3, f32[768,256]{1,0:T(8,128)} %pad_maximum_fusion.refs_3_), custom_call_target="tpu_custom_call" | custom-call | tf_op jit(solution)/shard_map/far_exchange_solve/pallas_call | solution.py:258
  208.4 2.0 convolution_subtract_fusion.1
  210.4 0.6 fusion.16
  211.1 0.6 fusion.5
  211.7 1.1 fusion.17
  212.8 1.0 fusion.4
  213.8 0.1 copy-done.2
  213.9 1.9 fusion.1
  215.8 2.5 fusion.18.g
  218.4 27.4 %sum_all_256.1.curv = f32[256,256]{1,0:T(8,128)} custom-call(f32[256,256]{1,0:T(8,128)} %fusion.18.g), custom_call_target="tpu_custom_call" | custom-call | tf_op jit(solution)/shard_map/sum_all_256/pallas_call | solution.py:373
  245.8 27.4 %second_step.1 = f32[256,256]{1,0:T(8,128)} custom-call(f32[256,256]{1,0:T(8,128)} %sum_all_256.1.curv, f32[256,256]{1,0:T(8,128)} %get-tuple-element.11.cur), custom_call_target="tpu_custom_call" | custom-call | tf_op jit(solution)/shard_map/second_step/pallas_call | solution.py:454
  273.2 3.0 %convolution_subtract_fusion = f32[1024,256]{1,0:T(8,128)} fusion(f32[1024,256]{1,0:T(8,128)S(1)} %convolution_subtract_fusion.1, f32[1024,256]{1,0:T(8,128)S(1)} %fusion.1, f32[256,256]{1,0:T(8,128)} %second_step.1), kind=kOutput, calls=%fused_computation.10 | convolution fusion | flops 805568512 | bytes 3407872 | tf_op jit(solution)/shard_map/dot_general | solution.py:500
  276.1 1.1 fusion.19
  277.3 2.8 %fusion.3 = f32[1024,256]{0,1:T(8,128)} fusion(f32[1024,256]{0,1:T(8,128)S(1)} %fusion.19, f32[256,256]{1,0:T(8,128)S(1)} %copy-done.5, f32[1024,256]{1,0:T(8,128)S(1)} %copy-done.1), kind=kOutput, calls=%fused_computation.8 | convolution fusion | flops 805568512 | bytes 3407872 | tf_op jit(solution)/shard_map/dot_general | solution.py:499
  280.1 2.5 copy.20
  (17 shorter events, 0.0 us)
Async XLA Ops:
  0.6 7.3 %copy-start = (f32[1024,512]{1,0:T(8,128)S(1)}, f32[1024,512]{1,0:T(8,128)}, u32[]{:S(2)}) copy-start(f32[1024,512]{1,0:T(8,128)} %param.10) | copy-start | bytes 6291460
  0.6 7.3 %copy-start.1 = (f32[1024,256]{1,0:T(8,128)S(1)}, f32[1024,256]{1,0:T(8,128)}, u32[]{:S(2)}) copy-start(f32[1024,256]{1,0:T(8,128)} %param.7) | copy-start | bytes 3145732
  73.6 2.1 copy-start.8
  208.3 2.1 copy-start.3
  208.3 2.1 copy-start.6
  208.3 2.7 copy-start.5
  208.4 2.7 copy-start.7
  211.7 2.2 copy-start.2
  273.2 3.0 %copy-start.4 = (f32[256,256]{1,0:T(8,128)S(1)}, f32[256,256]{1,0:T(8,128)}, u32[]{:S(2)}) copy-start(f32[256,256]{1,0:T(8,128)} %second_step.1) | copy-start | bytes 786436

commit v3 on v2

--- a/solution.py
+++ b/solution.py
@@ -34,11 +34,11 @@
 
 def far_kernel(n, solve, *refs):
     if solve:
-        meta, coef, c_hbm, grams, out, alpha, beta, updated = refs[:8]
-        refs = refs[8:]
+        meta, coef, c_hbm, grams, gram0, inverse0, out, alpha, beta, updated = refs[:10]
+        refs = refs[10:]
     else:
-        meta, coef, c_hbm, out = refs[:4]
-        refs = refs[4:]
+        meta, coef, c_hbm, grams, out, gram0, inverse0 = refs[:7]
+        refs = refs[7:]
     cv, ahead, ret, rs, ri, up, rz, c_sem, fs, fr, ss, sr, xs, xr, zs, zr = refs[:16]
     me = lax.axis_index("clu")
     z = me // GROUP
@@ -75,23 +75,7 @@
             return c
         lax.fori_loop(0, GROUP, zero, 0)
 
-    if solve:
-        greet_all(n, me)
-    else:
-        barrier = pltpu.get_barrier_semaphore()
-        pl.semaphore_signal(barrier, inc=1, device_id=(sib,), device_id_type=MESH)
-        for i in (1, 2, 3):
-            pl.semaphore_signal(barrier, inc=1, device_id=(base + chips[i] * 2 + k,), device_id_type=MESH)
-
-        @pl.when(has_up)
-        def _():
-            pl.semaphore_signal(barrier, inc=1, device_id=(me + GROUP,), device_id_type=MESH)
-
-        @pl.when(has_down)
-        def _():
-            pl.semaphore_signal(barrier, inc=1, device_id=(me - GROUP,), device_id_type=MESH)
-
-        pl.semaphore_wait(barrier, 4 + jnp.where(has_up, 1, 0) + jnp.where(has_down, 1, 0))
+    greet_all(n, me)
 
     f_z = rc(coef, ahead.at[p], fs.at[0], fr.at[0], me - GROUP)
 
@@ -130,9 +114,8 @@
     def _():
         f_s_own.start()
 
-    if solve:
-        total = refs[16]
-        finish_sum, drain_sum = start_sum(n, me, grams, total, *refs[17:])
+    total = refs[16]
+    finish_sum, drain_sum = start_sum(n, me, grams, total, *refs[17:])
 
     c_copy.wait()
 
@@ -172,9 +155,13 @@
         ret[t] = ret[t] + rs[i]
         r_x[i].start()
 
+    finish_sum()
     if solve:
-        finish_sum()
-        first_kernel(total, alpha, beta, updated)
+        first_steps(total, gram0, inverse0, alpha, beta, updated)
+    else:
+        g0 = symmetric(total[...])
+        gram0[...] = g0
+        inverse0[...] = invert([g0])[0]
 
     for i in (1, 2, 3):
         @pl.when(jnp.logical_or(chips[i] > a, has_up))
@@ -241,29 +228,27 @@
     def _():
         r_z.wait_send()
 
-    if solve:
-        drain_sum()
-
-
-def far_exchange(n, meta, coef_t, couplings, grams=None):
+    drain_sum()
+
+
+def far_exchange(n, meta, coef_t, couplings, grams, *first):
     blk = coef_t.shape
     f32 = jnp.float32
-    solve = grams is not None
+    solve = len(first) > 0
     vmem = pl.BlockSpec(memory_space=pltpu.VMEM)
     one = jax.ShapeDtypeStruct(blk, f32)
-    extra = []
-    if solve:
-        square = jax.ShapeDtypeStruct((grams.shape[1],) * 2, f32)
-        extra = [pltpu.VMEM(grams.shape, f32)] + sum_scratch(n, grams)
+    square = jax.ShapeDtypeStruct((grams.shape[1],) * 2, f32)
+    outs = (one,) + (square,) * (3 if solve else 2)
+    extra = [pltpu.VMEM(grams.shape, f32)] + sum_scratch(n, grams)
     return pl.pallas_call(
         functools.partial(far_kernel, n, solve),
-        out_shape=(one, square, square, square) if solve else one,
+        out_shape=outs,
         in_specs=[
             pl.BlockSpec(memory_space=pltpu.SMEM),
             pl.BlockSpec(memory_space=pltpu.VMEM),
             pl.BlockSpec(memory_space=pl.ANY),
-        ] + [vmem] * solve,
-        out_specs=(vmem,) * 4 if solve else vmem,
+        ] + [vmem] * (1 + len(first)),
+        out_specs=(vmem,) * len(outs),
         scratch_shapes=[
             pltpu.VMEM(couplings.shape, f32),
             pltpu.VMEM((GROUP,) + blk, f32),
@@ -285,7 +270,7 @@
         compiler_params=pltpu.CompilerParams(
             collective_id=int(solve), has_side_effects=True, vmem_limit_bytes=VMEM_LIMIT),
         name="far_exchange_solve" if solve else "far_exchange",
-    )(meta, coef_t, couplings, *([grams] if solve else []))
+    )(meta, coef_t, couplings, grams, *first)
 
 
 def greet_all(n, me):
@@ -430,19 +415,19 @@
     return 0.5 * (matrix + jnp.transpose(matrix))
 
 
-def first_kernel(grams, alpha_ref, beta_ref, updated_ref):
+def first_steps(grams, gram0, inverse0, alpha_ref, beta_ref, updated_ref):
     size = grams.shape[1]
-    g0 = symmetric(grams[:size, :])
-    g1 = symmetric(grams[size:2 * size, :])
-    g2 = symmetric(grams[2 * size:, :])
-    i0, i1 = invert([g0, g1])
+    g0 = gram0[...]
+    g1 = symmetric(grams[:size, :])
+    g2 = symmetric(grams[size:, :])
+    (i1,) = invert([g1])
     alpha = mm(i1, g0)
     alpha_ref[...] = alpha
     inner = mm(g2, alpha) - g1
     cross = mm(g1, alpha)
     updated = symmetric((g0 - cross) + mm(alpha, inner, contract_first))
     updated_ref[...] = updated
-    beta_ref[...] = mm(i0, updated)
+    beta_ref[...] = mm(inverse0[...], updated)
 
 
 def second_kernel(curv, cur, alpha_ref):
@@ -485,11 +470,12 @@
     def gram(x, y):
         return lax.dot_general(x, y, contract_first, precision=highest)
 
-    far_b = far_exchange(n, meta, coefficients(right_sides), couplings)
+    far_b, gram0, inverse0 = far_exchange(
+        n, meta, coefficients(right_sides), couplings, gram(right_sides, right_sides))
     image = image_of(right_sides, far_b)
-    local = jnp.concatenate([
-        gram(right_sides, right_sides), gram(right_sides, image), gram(image, image)])
-    far_w, alpha, beta, updated = far_exchange(n, meta, coefficients(image), couplings, local)
+    local = jnp.concatenate([gram(right_sides, image), gram(image, image)])
+    far_w, alpha, beta, updated = far_exchange(
+        n, meta, coefficients(image), couplings, local, gram0, inverse0)
     residual = right_sides - jnp.dot(image, alpha, precision=highest)
     direction = residual + jnp.dot(right_sides, beta, precision=highest)
     far_d = far_b + (gram(beta, far_b) - gram(alpha, far_w))

time: 283 us -> 308 us (1.088)
  Pallas kernels: 241 us -> 265 us
    pallas_call x2, Pallas kernels: 186 us -> 212 us  [far_exchange(): pl.pallas_call(functools.partial(far_kernel, n, solve), out_shape=outs, i...]
where the time goes in v3:
time: 308 us; the launch traced here: 307 us
  Pallas kernels  265 us (86%)
  matrix products  34.3 us (11%)
  other arithmetic  3.66 us (1%)
    pallas_call x2, Pallas kernels, far_exchange(): pl.pallas_call(functools.partial(far_kernel, n, solve), out_shape=outs, i...  212 us
    pallas_call x1, Pallas kernels, local_call(): pl.pallas_call(kernel, out_shape=out_shapes, compiler_params=pltpu.Compil...  27.3 us
    pallas_call x1, Pallas kernels, sum_all(): pl.pallas_call(functools.partial(sum_kernel, n), out_shape=jax.ShapeDtype...  26.1 us
    dot_general x6, matrix products, gram(): return lax.dot_general(x, y, contract_first, precision=highest)  11.5 us

profile of v3, /device:TPU:0, one launch (start us, length us, event | category | flops | bytes accessed | tf_op | source)
XLA Modules:
  0.0 307.3 jit_solution(7492340048945584003)
XLA Ops:
  0.6 0.0 copy-start
  1.5 0.8 fusion.8
  2.3 0.1 fusion.7
  2.4 0.7 and_select_fusion
  3.1 0.6 iota_reduce_fusion
  3.7 0.6 pad_add_fusion.refs_0_
  4.3 4.1 %fusion.13.refs_3_ = f32[256,256]{1,0:T(8,128)} fusion(f32[1024,256]{1,0:T(8,128)} %param.7), kind=kOutput, calls=%fused_computation.36 | convolution fusion | flops 805306368 | bytes 1310720 | tf_op jit(solution)/shard_map/dot_general | solution.py:471
  8.4 1.8 fusion.12.refs_1_
  10.2 97.7 %far_exchange.1 = (f32[256,512]{1,0:T(8,128)}, f32[256,256]{1,0:T(8,128)}, f32[256,256]{1,0:T(8,128)}) custom-call(s32[4,8]{1,0:T(4,128)} %pad_add_fusion.refs_0_, f32[256,512]{1,0:T(8,128)} %fusion.12.refs_1_, f32[6,512,512]{2,1,0:T(8,128)} %refs_2_.3, f32[256,256]{1,0:T(8,128)} %fusion.13.refs_3_), custom_call_target="tpu_custom_call" | custom-call | tf_op jit(solution)/shard_map/far_exchange/pallas_call | solution.py:243
  108.0 0.0 copy-start.8
  108.0 2.1 convolution_bitcast_fusion
  110.1 4.0 %fusion.2 = f32[1024,256]{1,0:T(8,128)S(1)} fusion(f32[1024,256]{1,0:T(8,128)S(1)} %convolution_bitcast_fusion, f32[1024,1024]{1,0:T(8,128)} %param.9, f32[1024,256]{1,0:T(8,128)S(1)} %copy-done.1, f32[1024]{0:T(1024)S(1)} %copy-done.8), kind=kOutput, calls=%fused_computation.7 | convolution fusion | flops 1611399168 | bytes 7344128 | tf_op jit(solution)/shard_map/dot_general | solution.py:466
  114.1 1.8 fusion.15
  116.0 1.8 convolution_bitcast_fusion.3
  117.8 0.8 pad_maximum_fusion.refs_3_
  118.6 1.8 fusion.14.refs_1_
  120.5 113.9 %far_exchange_solve.1 = (f32[256,512]{1,0:T(8,128)}, f32[256,256]{1,0:T(8,128)}, f32[256,256]{1,0:T(8,128)}, f32[256,256]{1,0:T(8,128)}) custom-call(s32[4,8]{1,0:T(4,128)} %pad_add_fusion.refs_0_, f32[256,512]{1,0:T(8,128)} %fusion.14.refs_1_, f32[6,512,512]{2,1,0:T(8,128)} %refs_2_.3, f32[512,256]{1,0:T(8,128)} %pad_maximum_fusion.refs_3_, ...), custom_call_target="tpu_custom_call" | custom-call | tf_op jit(solution)/shard_map/far_exchange_solve/pallas_call | solution.py:243
  234.4 2.0 convolution_subtract_fusion.1
  236.4 0.6 fusion.16
  237.1 0.6 fusion.5
  237.7 0.0 copy-start.2
  237.7 1.1 fusion.17
  238.8 1.0 fusion.4
  239.8 0.1 copy-done.2
  239.9 1.9 fusion.1
  241.8 2.5 fusion.18.g
  244.4 26.1 %sum_all_256.1.curv = f32[256,256]{1,0:T(8,128)} custom-call(f32[256,256]{1,0:T(8,128)} %fusion.18.g), custom_call_target="tpu_custom_call" | custom-call | tf_op jit(solution)/shard_map/sum_all_256/pallas_call | solution.py:358
  270.5 27.3 %second_step.1 = f32[256,256]{1,0:T(8,128)} custom-call(f32[256,256]{1,0:T(8,128)} %sum_all_256.1.curv, f32[256,256]{1,0:T(8,128)} %get-tuple-element.17.cur), custom_call_target="tpu_custom_call" | custom-call | tf_op jit(solution)/shard_map/second_step/pallas_call | solution.py:439
  297.8 3.0 convolution_subtract_fusion
  300.8 1.1 fusion.19
  301.9 2.8 fusion.3
  304.8 2.5 copy.20
  (17 shorter events, 0.0 us)
Async XLA Ops:
  0.6 7.8 %copy-start = (f32[1024,512]{1,0:T(8,128)S(1)}, f32[1024,512]{1,0:T(8,128)}, u32[]{:S(2)}) copy-start(f32[1024,512]{1,0:T(8,128)} %param.10) | copy-start | bytes 6291460
  0.6 7.8 %copy-start.1 = (f32[1024,256]{1,0:T(8,128)S(1)}, f32[1024,256]{1,0:T(8,128)}, u32[]{:S(2)}) copy-start(f32[1024,256]{1,0:T(8,128)} %param.7) | copy-start | bytes 3145732
  108.0 2.1 copy-start.8
  234.3 2.1 copy-start.3
  234.3 2.1 copy-start.6
  234.3 2.7 copy-start.5
  234.3 2.7 copy-start.7
  237.7 2.2 copy-start.2
  297.8 3.0 copy-start.4

commit v4 on v2

--- a/solution.py
+++ b/solution.py
@@ -174,7 +174,6 @@
 
     if solve:
         finish_sum()
-        first_kernel(total, alpha, beta, updated)
 
     for i in (1, 2, 3):
         @pl.when(jnp.logical_or(chips[i] > a, has_up))
@@ -196,6 +195,9 @@
     @pl.when(has_up)
     def _():
         r_z.start()
+
+    if solve:
+        first_kernel(total, alpha, beta, updated)
 
     for i in (1, 2, 3):
         @pl.when(jnp.logical_or(chips[i] > a, has_up))

time: 283 us -> 275 us (0.972)
  Pallas kernels: 241 us -> 232 us
    pallas_call x2, Pallas kernels: 186 us -> 179 us  [far_exchange(): pl.pallas_call(functools.partial(far_kernel, n, solve), out_shape=(one, s...]
where the time goes in v4:
time: 275 us; the launch traced here: 274 us
  Pallas kernels  232 us (84%)
  matrix products  33.8 us (12%)
  other arithmetic  3.76 us (1%)
    pallas_call x2, Pallas kernels, far_exchange(): pl.pallas_call(functools.partial(far_kernel, n, solve), out_shape=(one, s...  179 us
    pallas_call x1, Pallas kernels, local_call(): pl.pallas_call(kernel, out_shape=out_shapes, compiler_params=pltpu.Compil...  27.4 us
    pallas_call x1, Pallas kernels, sum_all(): pl.pallas_call(functools.partial(sum_kernel, n), out_shape=jax.ShapeDtype...  26.4 us
    dot_general x6, matrix products, gram(): return lax.dot_general(x, y, contract_first, precision=highest)  11.1 us
    dot_general x2, matrix products, image_of(): near = jnp.dot(near_block, vectors, precision=high)  5.94 us

profile of v4, /device:TPU:0, one launch (start us, length us, event | category | flops | bytes accessed | tf_op | source)
XLA Modules:
  0.0 274.4 jit_solution(1882065423077676456)
XLA Ops:
  0.6 0.0 copy-start
  0.6 0.0 copy-start.1
  1.5 0.8 fusion.8
  2.3 0.1 fusion.7
  2.4 0.7 and_select_fusion
  3.1 0.6 iota_reduce_fusion
  3.7 0.6 pad_add_fusion.refs_0_
  4.3 3.6 %fusion.14 = f32[256,256]{1,0:T(8,128)S(1)} fusion(f32[1024,256]{1,0:T(8,128)} %param.7), kind=kOutput, calls=%fused_computation.37 | convolution fusion | flops 805306368 | bytes 1310720 | tf_op jit(solution)/shard_map/dot_general | solution.py:488
  8.0 1.8 fusion.12.refs_1_
  9.8 63.8 %far_exchange.1 = f32[256,512]{1,0:T(8,128)} custom-call(s32[4,8]{1,0:T(4,128)} %pad_add_fusion.refs_0_, f32[256,512]{1,0:T(8,128)} %fusion.12.refs_1_, f32[6,512,512]{2,1,0:T(8,128)} %refs_2_.3), custom_call_target="tpu_custom_call" | custom-call | tf_op jit(solution)/shard_map/far_exchange/pallas_call | solution.py:260
  73.6 0.0 copy-start.8
  73.6 2.1 convolution_bitcast_fusion
  75.7 4.0 %fusion.2 = f32[1024,256]{1,0:T(8,128)S(1)} fusion(f32[1024,256]{1,0:T(8,128)S(1)} %convolution_bitcast_fusion, f32[1024,1024]{1,0:T(8,128)} %param.9, f32[1024,256]{1,0:T(8,128)S(1)} %copy-done.1, f32[1024]{0:T(1024)S(1)} %copy-done.8), kind=kOutput, calls=%fused_computation.7 | convolution fusion | flops 1611399168 | bytes 7344128 | tf_op jit(solution)/shard_map/dot_general | solution.py:483
  79.8 1.8 fusion.15
  81.6 1.8 convolution_bitcast_fusion.3
  83.5 0.9 pad_maximum_fusion.refs_3_
  84.4 1.8 fusion.13.refs_1_
  86.2 114.9 %far_exchange_solve.1 = (f32[256,512]{1,0:T(8,128)}, f32[256,256]{1,0:T(8,128)}, f32[256,256]{1,0:T(8,128)}, f32[256,256]{1,0:T(8,128)}) custom-call(s32[4,8]{1,0:T(4,128)} %pad_add_fusion.refs_0_, f32[256,512]{1,0:T(8,128)} %fusion.13.refs_1_, f32[6,512,512]{2,1,0:T(8,128)} %refs_2_.3, f32[768,256]{1,0:T(8,128)} %pad_maximum_fusion.refs_3_), custom_call_target="tpu_custom_call" | custom-call | tf_op jit(solution)/shard_map/far_exchange_solve/pallas_call | solution.py:260
  201.1 2.0 convolution_subtract_fusion.1
  203.2 0.6 fusion.16
  203.8 0.6 fusion.5
  204.5 1.1 fusion.17
  205.6 1.0 fusion.4
  206.6 0.1 copy-done.2
  206.7 1.9 fusion.1
  208.6 2.5 fusion.18.g
  211.1 26.4 %sum_all_256.1.curv = f32[256,256]{1,0:T(8,128)} custom-call(f32[256,256]{1,0:T(8,128)} %fusion.18.g), custom_call_target="tpu_custom_call" | custom-call | tf_op jit(solution)/shard_map/sum_all_256/pallas_call | solution.py:375
  237.5 27.4 %second_step.1 = f32[256,256]{1,0:T(8,128)} custom-call(f32[256,256]{1,0:T(8,128)} %sum_all_256.1.curv, f32[256,256]{1,0:T(8,128)} %get-tuple-element.11.cur), custom_call_target="tpu_custom_call" | custom-call | tf_op jit(solution)/shard_map/second_step/pallas_call | solution.py:456
  264.9 3.0 %convolution_subtract_fusion = f32[1024,256]{1,0:T(8,128)} fusion(f32[1024,256]{1,0:T(8,128)S(1)} %convolution_subtract_fusion.1, f32[1024,256]{1,0:T(8,128)S(1)} %fusion.1, f32[256,256]{1,0:T(8,128)} %second_step.1), kind=kOutput, calls=%fused_computation.10 | convolution fusion | flops 805568512 | bytes 3407872 | tf_op jit(solution)/shard_map/dot_general | solution.py:502
  267.9 1.1 fusion.19
  269.0 2.8 %fusion.3 = f32[1024,256]{0,1:T(8,128)} fusion(f32[1024,256]{0,1:T(8,128)S(1)} %fusion.19, f32[256,256]{1,0:T(8,128)S(1)} %copy-done.5, f32[1024,256]{1,0:T(8,128)S(1)} %copy-done.1), kind=kOutput, calls=%fused_computation.8 | convolution fusion | flops 805568512 | bytes 3407872 | tf_op jit(solution)/shard_map/dot_general | solution.py:501
  271.9 2.5 copy.20
  (17 shorter events, 0.0 us)
Async XLA Ops:
  0.6 7.3 %copy-start = (f32[1024,512]{1,0:T(8,128)S(1)}, f32[1024,512]{1,0:T(8,128)}, u32[]{:S(2)}) copy-start(f32[1024,512]{1,0:T(8,128)} %param.10) | copy-start | bytes 6291460
  0.6 7.3 %copy-start.1 = (f32[1024,256]{1,0:T(8,128)S(1)}, f32[1024,256]{1,0:T(8,128)}, u32[]{:S(2)}) copy-start(f32[1024,256]{1,0:T(8,128)} %param.7) | copy-start | bytes 3145732
  73.6 2.1 copy-start.8
  201.1 2.1 copy-start.3
  201.1 2.1 copy-start.6
  201.1 2.7 copy-start.5
  201.1 2.7 copy-start.7
  204.5 2.2 copy-start.2
  264.9 3.0 %copy-start.4 = (f32[256,256]{1,0:T(8,128)S(1)}, f32[256,256]{1,0:T(8,128)}, u32[]{:S(2)}) copy-start(f32[256,256]{1,0:T(8,128)} %second_step.1) | copy-start | bytes 786436
